TPU v7x, 32 devices: a whole 2x2x4 slice. The times are simulated.
32 devices in a mesh: rep: 2 (over x), rank: 16 (over z, y, core).
Axes of the slice: x: 2, y: 2, z: 4, core: 2. Of those that a mesh axis runs over, the one named last changes fastest.
Arguments:
- tokens: bfloat16 [4096, 2048], P(('rep', 'rank')), parts along dimension 0, may hold values from -6 to 6
- routes: int32 [4096, 8], P(('rep', 'rank')), parts along dimension 0, may hold values from 0 to 15, all different within a row; in each aligned block of 32 rows (0 to 31, 32 to 63, ...) at most 24 rows name the same one
- gate_weights: float32 [4096, 8], P(('rep', 'rank')), parts along dimension 0, may hold values from 0.05 to 0.5
- token_order: int32 [128, 32], P(('rep', 'rank')), parts along dimension 0, may hold values from 0 to 31, each once within a row
- w_gate: bfloat16 [16, 2048, 768], P('rank'), may hold values from -0.125 to 0.125
- w_up: bfloat16 [16, 2048, 768], P('rank'), may hold values from -0.125 to 0.125
- w_down: bfloat16 [16, 768, 2048], P('rank'), may hold values from -0.21875 to 0.21875
Outputs:
- mixed: bfloat16 [4096, 2048], P(('rep', 'rank')), parts along dimension 0
There are 2 independent parts, one for each index of `rep`. A program takes and returns all parts, laid end to end along the dimension named above; an argument that names none is the same for every part. Nothing has to cross between parts.
Inputs may be any that keep to these rules, and one draw needn't show every extreme that they name: `routes`: each row names 8 different experts; every expert is named somewhere. In each aligned block of 32 rows no expert is named by more than 24 rows, and in every draw some block has an expert named by exactly 24 rows. `token_order`: each row is a permutation of the 32 row numbers of a block.
All inputs are finite; a program needn't handle non-finite values.
Results may differ from a plain program's by a relative error of at most 0.0058.
Values may be sent and summed in bfloat16 or wider, within the bound.
A program may use at most 128 MiB of HBM per device.

v0:
```python
import jax
import jax.numpy as jnp
from jax import lax
from jax.sharding import PartitionSpec as P


def layout(route_rows, gate_rows, experts, slot_count, offset):
    row_total = route_rows.shape[0]
    picks = route_rows.shape[1]
    flat_routes = route_rows.reshape(-1)
    onehot = (flat_routes[:, None] == jnp.arange(experts, dtype=jnp.int32)[None, :]).astype(
        jnp.int32
    )
    before = jnp.cumsum(onehot, axis=0) - onehot
    slot_index = jnp.sum(before * onehot, axis=1)
    target = flat_routes * slot_count + offset + slot_index
    columns = jnp.arange(experts * slot_count, dtype=jnp.int32)
    matched = (target[:, None] == columns[None, :]).astype(jnp.float32)
    matched = matched.reshape(row_total, picks, experts * slot_count)
    dispatch = jnp.sum(matched, axis=1).astype(jnp.bfloat16)
    collect = jnp.sum(matched * gate_rows[:, :, None], axis=1)
    return (dispatch, collect)


def per_device(tokens, routes, gate_weights, token_order, w_gate, w_up, w_down):
    experts = lax.axis_size("rank")
    blocks, block_rows = token_order.shape
    picks = routes.shape[1]
    features = tokens.shape[1]
    capacity = max(2, 3 * block_rows * picks // (2 * experts))
    pieces = []
    for block_index in range(blocks):
        lower = block_index * block_rows
        upper = lower + block_rows
        dispatch, collect = layout(
            routes[lower:upper], gate_weights[lower:upper], experts, capacity, 0
        )
        outgoing = jnp.einsum(
            "cs,cd->sd", dispatch, tokens[lower:upper], preferred_element_type=jnp.float32
        )
        outgoing = outgoing.astype(jnp.bfloat16).reshape(experts, capacity, features)
        arrived = lax.all_to_all(outgoing, "rank", split_axis=0, concat_axis=0, tiled=True)
        sources, slot_run, width_in = arrived.shape
        flat_rows = arrived.reshape(-1, width_in)
        gate_proj = jnp.dot(flat_rows, w_gate[0], preferred_element_type=jnp.float32)
        up_proj = jnp.dot(flat_rows, w_up[0], preferred_element_type=jnp.float32)
        hidden = (jax.nn.silu(gate_proj) * up_proj).astype(jnp.bfloat16)
        expert_out = jnp.dot(hidden, w_down[0], preferred_element_type=jnp.float32).astype(
            jnp.bfloat16
        )
        expert_out = expert_out.reshape(sources, slot_run, width_in)
        returned = lax.all_to_all(expert_out, "rank", split_axis=0, concat_axis=0, tiled=True)
        flat_back = returned.reshape(-1, features).astype(jnp.float32)
        summed = jnp.dot(collect, flat_back, precision=lax.Precision.HIGHEST)
        rounded = summed.astype(jnp.bfloat16)
        pieces.append(jnp.take(rounded, token_order[block_index], axis=0))
    return jnp.concatenate(pieces, axis=0)


def solution(mesh):
    return jax.shard_map(
        per_device,
        mesh=mesh,
        in_specs=(
            P(("rep", "rank"), None),
            P(("rep", "rank"), None),
            P(("rep", "rank"), None),
            P(("rep", "rank"), None),
            P("rank", None, None),
            P("rank", None, None),
            P("rank", None, None),
        ),
        out_specs=P(("rep", "rank"), None),
        check_vma=False,
    )
```

profile of v0, /device:TPU:8, one launch (start us, length us, event | category | flops | bytes accessed | tf_op | source)
XLA Modules:
  0.0 342.1 jit_solution(3378726837794947345)
XLA Ops:
  0.0 1.0 fusion.101
  1.2 0.6 reduce-window.36
  2.2 0.9 fusion.100
  3.5 2.6 convolution_convert_fusion
  6.2 6.3 %all-to-all-start.6 = ((bf16[16,24,2048]{2,1,0:T(8,128)(2,1)}), bf16[16,24,2048]{2,1,0:T(8,128)(2,1)}, u32[]{:S(2)}, u32[]{:S(2)}) async-start(bf16[16,24,2048]{2,1,0:T(8,128)(2,1)} %bitcast.185), calls=%async_computation.6 | async-start | bytes 3145728 | tf_op jit(solution)/shard_map/all_to_all | solution.py:42
  12.8 0.6 reduce-window.34
  14.2 2.6 convolution_convert_fusion.1
  16.8 30.6 %all-to-all-done.6 = bf16[16,24,2048]{2,1,0:T(8,128)(2,1)} async-done(((bf16[16,24,2048]{2,1,0:T(8,128)(2,1)}), bf16[16,24,2048]{2,1,0:T(8,128)(2,1)}, u32[]{:S(2)}, u32[]{:S(2)}) %all-to-all-start.6) | async-done | bytes 1572896 | tf_op jit(solution)/shard_map/all_to_all | solution.py:42
  47.4 6.3 %all-to-all-start.4 = ((bf16[16,24,2048]{2,1,0:T(8,128)(2,1)}), bf16[16,24,2048]{2,1,0:T(8,128)(2,1)}, u32[]{:S(2)}, u32[]{:S(2)}) async-start(bf16[16,24,2048]{2,1,0:T(8,128)(2,1)} %bitcast.184), calls=%async_computation.4 | async-start | bytes 3145728 | tf_op jit(solution)/shard_map/all_to_all | solution.py:42
  54.0 0.6 reduce-window.30
  55.0 0.9 convert_reduce_fusion.2
  56.0 2.6 convolution_convert_fusion.2
  58.6 30.0 %all-to-all-done.4 = bf16[16,24,2048]{2,1,0:T(8,128)(2,1)} async-done(((bf16[16,24,2048]{2,1,0:T(8,128)(2,1)}), bf16[16,24,2048]{2,1,0:T(8,128)(2,1)}, u32[]{:S(2)}, u32[]{:S(2)}) %all-to-all-start.4) | async-done | bytes 1572896 | tf_op jit(solution)/shard_map/all_to_all | solution.py:42
  88.6 6.3 %all-to-all-start.2 = ((bf16[16,24,2048]{2,1,0:T(8,128)(2,1)}), bf16[16,24,2048]{2,1,0:T(8,128)(2,1)}, u32[]{:S(2)}, u32[]{:S(2)}) async-start(bf16[16,24,2048]{2,1,0:T(8,128)(2,1)} %bitcast.183), calls=%async_computation.2 | async-start | bytes 3145728 | tf_op jit(solution)/shard_map/all_to_all | solution.py:42
  95.2 0.6 reduce-window.26
  96.2 0.9 convert_reduce_fusion.3
  97.2 2.7 convolution_convert_fusion.3
  99.9 29.9 %all-to-all-done.2 = bf16[16,24,2048]{2,1,0:T(8,128)(2,1)} async-done(((bf16[16,24,2048]{2,1,0:T(8,128)(2,1)}), bf16[16,24,2048]{2,1,0:T(8,128)(2,1)}, u32[]{:S(2)}, u32[]{:S(2)}) %all-to-all-start.2) | async-done | bytes 1572896 | tf_op jit(solution)/shard_map/all_to_all | solution.py:42
  129.8 6.3 %all-to-all-start = ((bf16[16,24,2048]{2,1,0:T(8,128)(2,1)}), bf16[16,24,2048]{2,1,0:T(8,128)(2,1)}, u32[]{:S(2)}, u32[]{:S(2)}) async-start(bf16[16,24,2048]{2,1,0:T(8,128)(2,1)} %bitcast.186), calls=%async_computation | async-start | bytes 3145728 | tf_op jit(solution)/shard_map/all_to_all | solution.py:42
  136.1 4.7 %fusion.16 = f32[384,768]{1,0:T(8,128)} fusion(bf16[384,2048]{1,0:T(8,128)(2,1)} %bitcast.24, bf16[1,2048,768]{2,1,0:T(8,128)(2,1)} %param.13), kind=kOutput, calls=%fused_computation.20 | convolution fusion | flops 1207959552 | bytes 5898240 | tf_op jit(solution)/shard_map/dot_general | solution.py:45
  140.8 6.9 %fusion.33 = bf16[384,2048]{1,0:T(8,128)(2,1)} fusion(bf16[1,768,2048]{2,1,0:T(8,128)(2,1)S(1)} %copy-done, bf16[384,2048]{1,0:T(8,128)(2,1)} %bitcast.24, bf16[1,2048,768]{2,1,0:T(8,128)(2,1)} %param.14, f32[384,768]{1,0:T(8,128)} %fusion.16), kind=kOutput, calls=%fused_computation.31 | convolution fusion | flops 2418475008 | bytes 10616832 | tf_op jit(solution)/shard_map/dot_general | solution.py:48
  147.7 23.3 %all-to-all-done = bf16[16,24,2048]{2,1,0:T(8,128)(2,1)} async-done(((bf16[16,24,2048]{2,1,0:T(8,128)(2,1)}), bf16[16,24,2048]{2,1,0:T(8,128)(2,1)}, u32[]{:S(2)}, u32[]{:S(2)}) %all-to-all-start) | async-done | bytes 1572896 | tf_op jit(solution)/shard_map/all_to_all | solution.py:42
  171.0 6.3 %all-to-all-start.7 = ((bf16[16,24,2048]{2,1,0:T(8,128)(2,1)}), bf16[16,24,2048]{2,1,0:T(8,128)(2,1)}, u32[]{:S(2)}, u32[]{:S(2)}) async-start(bf16[16,24,2048]{2,1,0:T(8,128)(2,1)} %bitcast.188), calls=%async_computation.7 | async-start | bytes 3145728 | tf_op jit(solution)/shard_map/all_to_all | solution.py:52
  177.3 4.7 %fusion.18 = f32[384,768]{1,0:T(8,128)} fusion(bf16[384,2048]{1,0:T(8,128)(2,1)} %bitcast.18, bf16[1,2048,768]{2,1,0:T(8,128)(2,1)} %param.13), kind=kOutput, calls=%fused_computation.22 | convolution fusion | flops 1207959552 | bytes 5898240 | tf_op jit(solution)/shard_map/dot_general | solution.py:45
  182.0 7.0 %fusion.30 = bf16[384,2048]{1,0:T(8,128)(2,1)} fusion(bf16[1,768,2048]{2,1,0:T(8,128)(2,1)S(1)} %copy-done, bf16[384,2048]{1,0:T(8,128)(2,1)} %bitcast.18, bf16[1,2048,768]{2,1,0:T(8,128)(2,1)} %param.14, f32[384,768]{1,0:T(8,128)} %fusion.18), kind=kOutput, calls=%fused_computation.30 | convolution fusion | flops 2418475008 | bytes 10616832 | tf_op jit(solution)/shard_map/dot_general | solution.py:48
  189.0 23.2 %all-to-all-done.7 = bf16[16,24,2048]{2,1,0:T(8,128)(2,1)} async-done(((bf16[16,24,2048]{2,1,0:T(8,128)(2,1)}), bf16[16,24,2048]{2,1,0:T(8,128)(2,1)}, u32[]{:S(2)}, u32[]{:S(2)}) %all-to-all-start.7) | async-done | bytes 1572896 | tf_op jit(solution)/shard_map/all_to_all | solution.py:52
  212.2 6.3 %all-to-all-start.5 = ((bf16[16,24,2048]{2,1,0:T(8,128)(2,1)}), bf16[16,24,2048]{2,1,0:T(8,128)(2,1)}, u32[]{:S(2)}, u32[]{:S(2)}) async-start(bf16[16,24,2048]{2,1,0:T(8,128)(2,1)} %bitcast.189), calls=%async_computation.5 | async-start | bytes 3145728 | tf_op jit(solution)/shard_map/all_to_all | solution.py:52
  218.5 4.8 %fusion.20 = f32[384,768]{1,0:T(8,128)} fusion(bf16[384,2048]{1,0:T(8,128)(2,1)} %bitcast.12, bf16[1,2048,768]{2,1,0:T(8,128)(2,1)} %param.13), kind=kOutput, calls=%fused_computation.24 | convolution fusion | flops 1207959552 | bytes 5898240 | tf_op jit(solution)/shard_map/dot_general | solution.py:45
  223.3 6.9 %fusion.27 = bf16[384,2048]{1,0:T(8,128)(2,1)} fusion(bf16[1,768,2048]{2,1,0:T(8,128)(2,1)S(1)} %copy-done, bf16[384,2048]{1,0:T(8,128)(2,1)} %bitcast.12, bf16[1,2048,768]{2,1,0:T(8,128)(2,1)} %param.14, f32[384,768]{1,0:T(8,128)} %fusion.20), kind=kOutput, calls=%fused_computation.29 | convolution fusion | flops 2418475008 | bytes 10616832 | tf_op jit(solution)/shard_map/dot_general | solution.py:48
  230.2 23.3 %all-to-all-done.5 = bf16[16,24,2048]{2,1,0:T(8,128)(2,1)} async-done(((bf16[16,24,2048]{2,1,0:T(8,128)(2,1)}), bf16[16,24,2048]{2,1,0:T(8,128)(2,1)}, u32[]{:S(2)}, u32[]{:S(2)}) %all-to-all-start.5) | async-done | bytes 1572896 | tf_op jit(solution)/shard_map/all_to_all | solution.py:52
  253.4 6.3 %all-to-all-start.3 = ((bf16[16,24,2048]{2,1,0:T(8,128)(2,1)}), bf16[16,24,2048]{2,1,0:T(8,128)(2,1)}, u32[]{:S(2)}, u32[]{:S(2)}) async-start(bf16[16,24,2048]{2,1,0:T(8,128)(2,1)} %bitcast.190), calls=%async_computation.3 | async-start | bytes 3145728 | tf_op jit(solution)/shard_map/all_to_all | solution.py:52
  259.7 4.9 %fusion.22 = f32[384,768]{1,0:T(8,128)} fusion(bf16[384,2048]{1,0:T(8,128)(2,1)} %bitcast.3, bf16[1,2048,768]{2,1,0:T(8,128)(2,1)} %param.13), kind=kOutput, calls=%fused_computation.26 | convolution fusion | flops 1207959552 | bytes 5898240 | tf_op jit(solution)/shard_map/dot_general | solution.py:45
  264.6 6.9 %fusion.24 = bf16[384,2048]{1,0:T(8,128)(2,1)} fusion(bf16[1,768,2048]{2,1,0:T(8,128)(2,1)S(1)} %copy-done, bf16[384,2048]{1,0:T(8,128)(2,1)} %bitcast.3, bf16[1,2048,768]{2,1,0:T(8,128)(2,1)} %param.14, f32[384,768]{1,0:T(8,128)} %fusion.22), kind=kOutput, calls=%fused_computation.28 | convolution fusion | flops 2418475008 | bytes 10616832 | tf_op jit(solution)/shard_map/dot_general | solution.py:48
  271.4 23.2 %all-to-all-done.3 = bf16[16,24,2048]{2,1,0:T(8,128)(2,1)} async-done(((bf16[16,24,2048]{2,1,0:T(8,128)(2,1)}), bf16[16,24,2048]{2,1,0:T(8,128)(2,1)}, u32[]{:S(2)}, u32[]{:S(2)}) %all-to-all-start.3) | async-done | bytes 1572896 | tf_op jit(solution)/shard_map/all_to_all | solution.py:52
  294.6 6.4 %all-to-all-start.1 = ((bf16[16,24,2048]{2,1,0:T(8,128)(2,1)}), bf16[16,24,2048]{2,1,0:T(8,128)(2,1)}, u32[]{:S(2)}, u32[]{:S(2)}) async-start(bf16[16,24,2048]{2,1,0:T(8,128)(2,1)} %bitcast.187), calls=%async_computation.1 | async-start | bytes 3145728 | tf_op jit(solution)/shard_map/all_to_all | solution.py:52
  301.0 0.6 compare_and_fusion.3
  301.6 2.3 convolution_convert_fusion.4
  303.9 0.7 gather_fusion.3
  304.6 2.3 convolution_convert_fusion.5
  306.8 0.7 gather_fusion.2
  307.5 2.3 convolution_convert_fusion.6
  309.8 1.3 gather_fusion.1
  311.1 24.9 %all-to-all-done.1 = bf16[16,24,2048]{2,1,0:T(8,128)(2,1)} async-done(((bf16[16,24,2048]{2,1,0:T(8,128)(2,1)}), bf16[16,24,2048]{2,1,0:T(8,128)(2,1)}, u32[]{:S(2)}, u32[]{:S(2)}) %all-to-all-start.1) | async-done | bytes 1572896 | tf_op jit(solution)/shard_map/all_to_all | solution.py:52
  335.9 2.3 convolution_convert_fusion.7
  338.2 1.3 gather_fusion
  339.5 0.7 broadcast_select_fusion
  340.2 1.1 broadcast_select_fusion.2
  341.3 0.8 pad_maximum_fusion
  (58 shorter events, 3.6 us)
Async XLA Ops:
  0.0 140.8 %copy-start = (bf16[1,768,2048]{2,1,0:T(8,128)(2,1)S(1)}, bf16[1,768,2048]{2,1,0:T(8,128)(2,1)}, u32[]{:S(2)}) copy-start(bf16[1,768,2048]{2,1,0:T(8,128)(2,1)} %param.15) | copy-start | bytes 9437188
  6.2 41.2 %all-to-all-start.6 = ((bf16[16,24,2048]{2,1,0:T(8,128)(2,1)}), bf16[16,24,2048]{2,1,0:T(8,128)(2,1)}, u32[]{:S(2)}, u32[]{:S(2)}) async-start(bf16[16,24,2048]{2,1,0:T(8,128)(2,1)} %bitcast.185), calls=%async_computation.6 | async-start | bytes 3145728 | tf_op jit(solution)/shard_map/all_to_all | solution.py:42
  47.4 41.2 %all-to-all-start.4 = ((bf16[16,24,2048]{2,1,0:T(8,128)(2,1)}), bf16[16,24,2048]{2,1,0:T(8,128)(2,1)}, u32[]{:S(2)}, u32[]{:S(2)}) async-start(bf16[16,24,2048]{2,1,0:T(8,128)(2,1)} %bitcast.184), calls=%async_computation.4 | async-start | bytes 3145728 | tf_op jit(solution)/shard_map/all_to_all | solution.py:42
  88.6 41.2 %all-to-all-start.2 = ((bf16[16,24,2048]{2,1,0:T(8,128)(2,1)}), bf16[16,24,2048]{2,1,0:T(8,128)(2,1)}, u32[]{:S(2)}, u32[]{:S(2)}) async-start(bf16[16,24,2048]{2,1,0:T(8,128)(2,1)} %bitcast.183), calls=%async_computation.2 | async-start | bytes 3145728 | tf_op jit(solution)/shard_map/all_to_all | solution.py:42
  129.8 41.2 %all-to-all-start = ((bf16[16,24,2048]{2,1,0:T(8,128)(2,1)}), bf16[16,24,2048]{2,1,0:T(8,128)(2,1)}, u32[]{:S(2)}, u32[]{:S(2)}) async-start(bf16[16,24,2048]{2,1,0:T(8,128)(2,1)} %bitcast.186), calls=%async_computation | async-start | bytes 3145728 | tf_op jit(solution)/shard_map/all_to_all | solution.py:42
  171.0 41.2 %all-to-all-start.7 = ((bf16[16,24,2048]{2,1,0:T(8,128)(2,1)}), bf16[16,24,2048]{2,1,0:T(8,128)(2,1)}, u32[]{:S(2)}, u32[]{:S(2)}) async-start(bf16[16,24,2048]{2,1,0:T(8,128)(2,1)} %bitcast.188), calls=%async_computation.7 | async-start | bytes 3145728 | tf_op jit(solution)/shard_map/all_to_all | solution.py:52
  212.2 41.2 %all-to-all-start.5 = ((bf16[16,24,2048]{2,1,0:T(8,128)(2,1)}), bf16[16,24,2048]{2,1,0:T(8,128)(2,1)}, u32[]{:S(2)}, u32[]{:S(2)}) async-start(bf16[16,24,2048]{2,1,0:T(8,128)(2,1)} %bitcast.189), calls=%async_computation.5 | async-start | bytes 3145728 | tf_op jit(solution)/shard_map/all_to_all | solution.py:52
  253.4 41.2 %all-to-all-start.3 = ((bf16[16,24,2048]{2,1,0:T(8,128)(2,1)}), bf16[16,24,2048]{2,1,0:T(8,128)(2,1)}, u32[]{:S(2)}, u32[]{:S(2)}) async-start(bf16[16,24,2048]{2,1,0:T(8,128)(2,1)} %bitcast.190), calls=%async_computation.3 | async-start | bytes 3145728 | tf_op jit(solution)/shard_map/all_to_all | solution.py:52
  294.6 6.4 %copy-start.1 = (s32[4,32]{1,0:T(4,128)S(1)}, s32[4,32]{1,0:T(4,128)}, u32[]{:S(2)}) copy-start(s32[4,32]{1,0:T(4,128)} %param.12) | copy-start | bytes 1540
  294.6 41.3 %all-to-all-start.1 = ((bf16[16,24,2048]{2,1,0:T(8,128)(2,1)}), bf16[16,24,2048]{2,1,0:T(8,128)(2,1)}, u32[]{:S(2)}, u32[]{:S(2)}) async-start(bf16[16,24,2048]{2,1,0:T(8,128)(2,1)} %bitcast.187), calls=%async_computation.1 | async-start | bytes 3145728 | tf_op jit(solution)/shard_map/all_to_all | solution.py:52
  311.1 28.4 %copy-start.3 = (pred[32]{0:T(512)(128)(4,1)S(1)}, pred[32]{0:T(512)(128)(4,1)}, u32[]{:S(2)}) copy-start(pred[32]{0:T(512)(128)(4,1)} %get-tuple-element.32) | copy-start | bytes 100
  335.9 4.3 %copy-start.2 = (pred[32]{0:T(512)(128)(4,1)S(1)}, pred[32]{0:T(512)(128)(4,1)}, u32[]{:S(2)}) copy-start(pred[32]{0:T(512)(128)(4,1)} %get-tuple-element.30) | copy-start | bytes 100
where the time goes:
time: 345 us; the launch traced here: 342 us
  waiting for transfers between devices  208 us (60%)
  matrix products  66.5 us (19%)
  starting transfers between devices  50.3 us (15%)
  other arithmetic  8.58 us (2%)
  local copies, waits for them, and re-layouts  8.19 us (2%)
    all_to_all x4, waiting for transfers between devices, per_device(): lax.all_to_all(outgoing, 'rank', split_axis=0, concat_axis=0, tiled=True)  114 us
    all_to_all x4, waiting for transfers between devices, per_device(): lax.all_to_all(expert_out, 'rank', split_axis=0, concat_axis=0, tiled=True)  94.5 us
    dot_general x4, matrix products, per_device(): jnp.dot(hidden, w_down[0], preferred_element_type=jnp.float32)  27.6 us
    all_to_all x4, starting transfers between devices, per_device(): lax.all_to_all(expert_out, 'rank', split_axis=0, concat_axis=0, tiled=True)  25.2 us
    all_to_all x4, starting transfers between devices, per_device(): lax.all_to_all(outgoing, 'rank', split_axis=0, concat_axis=0, tiled=True)  25.1 us
    dot_general x4, matrix products, per_device(): jnp.dot(flat_rows, w_gate[0], preferred_element_type=jnp.float32)  19.1 us
    dot_general x4, matrix products, per_device(): jnp.einsum('cs,cd->sd', dispatch, tokens[lower:upper], preferred_element_...  10.7 us
    dot_general x4, matrix products, per_device(): summed = jnp.dot(collect, flat_back, precision=lax.Precision.HIGHEST)  9.1 us
  transfers between devices with their start and end apart: 8, of which 8 were waited for; matrix products, arithmetic and copies ran while one was open for 21% of the time, Pallas kernels for 0%

commit v1 on v0

v1 whole, which is shorter than its diff:
```python
import jax
import jax.numpy as jnp
from jax import lax
from jax.sharding import PartitionSpec as P


def per_device(tokens, routes, gate_weights, token_order, w_gate, w_up, w_down):
    rank = lax.axis_index("rank")
    rows, features = tokens.shape
    blocks, block_rows = token_order.shape

    everyone = lax.all_gather(tokens, "rank", axis=0, tiled=True)
    all_routes = lax.all_gather(routes, "rank", axis=0, tiled=True)
    all_gates = lax.all_gather(gate_weights, "rank", axis=0, tiled=True)
    factor = jnp.sum(jnp.where(all_routes == rank, all_gates, 0.0), axis=1)

    gate_proj = jnp.dot(everyone, w_gate[0], preferred_element_type=jnp.float32)
    up_proj = jnp.dot(everyone, w_up[0], preferred_element_type=jnp.float32)
    hidden = (jax.nn.silu(gate_proj) * up_proj).astype(jnp.bfloat16)
    expert_out = jnp.dot(hidden, w_down[0], preferred_element_type=jnp.float32)
    weighed = (factor[:, None] * expert_out).astype(jnp.bfloat16)
    combined = lax.psum_scatter(weighed, "rank", scatter_dimension=0, tiled=True)

    order = token_order + jnp.arange(blocks, dtype=jnp.int32)[:, None] * block_rows
    pick = (order.reshape(-1)[:, None] == jnp.arange(rows, dtype=jnp.int32)[None, :])
    return jnp.dot(
        pick.astype(jnp.bfloat16), combined, preferred_element_type=jnp.float32
    ).astype(jnp.bfloat16)


def solution(mesh):
    return jax.shard_map(
        per_device,
        mesh=mesh,
        in_specs=(
            P(("rep", "rank"), None),
            P(("rep", "rank"), None),
            P(("rep", "rank"), None),
            P(("rep", "rank"), None),
            P("rank", None, None),
            P("rank", None, None),
            P("rank", None, None),
        ),
        out_specs=P(("rep", "rank"), None),
        check_vma=False,
    )
```

time: 345 us -> 232 us (0.67)
  waiting for transfers between devices: 208 us -> 144 us
  starting transfers between devices: 50.3 us -> 0.04 us
  blocking collectives: 0 us -> 37.6 us
  matrix products: 66.5 us -> 34.5 us
  between operations: 0.19 us -> 13.4 us
  other arithmetic: 8.58 us -> 0.1 us
  local copies, waits for them, and re-layouts: 8.19 us -> 0.74 us
    all_to_all x8 -> x0, waiting for transfers between devices: 208 us -> none  [the longest x4 114 us: per_device(): lax.all_to_all(outgoing, 'rank', split_axis=0, concat_axis=0, tiled=True)]
    reduce_scatter x0 -> x1, waiting for transfers between devices: none -> 103 us  [per_device(): lax.psum_scatter(weighed, 'rank', scatter_dimension=0, tiled=True)]
    all_to_all x8 -> x0, starting transfers between devices: 50.3 us -> none  [the longest x4 25.2 us: per_device(): lax.all_to_all(expert_out, 'rank', split_axis=0, concat_axis=0, tiled=True)]
    all_gather x0 -> x1, waiting for transfers between devices: none -> 40.4 us  [per_device(): everyone = lax.all_gather(tokens, 'rank', axis=0, tiled=True)]
    all_gather x0 -> x2, blocking collectives: none -> 37.6 us  [the longest x1 19.5 us: per_device(): all_gates = lax.all_gather(gate_weights, 'rank', axis=0, tiled=True)]
    dot_general x16 -> x3, matrix products: 66.5 us -> 34.5 us  [the longest x1 20.6 us: per_device(): expert_out = jnp.dot(hidden, w_down[0], preferred_element_type=jnp.float32)]
    gather x4 -> x0, local copies, waits for them, and re-layouts: 3.89 us -> none  [per_device(): pieces.append(jnp.take(rounded, token_order[block_index], axis=0))]
  transfers between devices with their start and end apart: 8 -> 2, of which waited for: 8 -> 2; matrix products, arithmetic and copies ran while one was open for 21% -> 0% of each run, Pallas kernels for 0% -> 0%
where the time goes in v1:
time: 232 us; the launch traced here: 230 us
  waiting for transfers between devices  144 us (62%)
  blocking collectives  37.6 us (16%)
  matrix products  34.5 us (15%)
  between operations  13.4 us (6%)
    reduce_scatter x1, waiting for transfers between devices, per_device(): lax.psum_scatter(weighed, 'rank', scatter_dimension=0, tiled=True)  103 us
    all_gather x1, waiting for transfers between devices, per_device(): everyone = lax.all_gather(tokens, 'rank', axis=0, tiled=True)  40.4 us
    dot_general x1, matrix products, per_device(): expert_out = jnp.dot(hidden, w_down[0], preferred_element_type=jnp.float32)  20.6 us
    all_gather x1, blocking collectives, per_device(): all_gates = lax.all_gather(gate_weights, 'rank', axis=0, tiled=True)  19.5 us
    all_gather x1, blocking collectives, per_device(): all_routes = lax.all_gather(routes, 'rank', axis=0, tiled=True)  18 us
    dot_general x1, matrix products, per_device(): gate_proj = jnp.dot(everyone, w_gate[0], preferred_element_type=jnp.float32)  11.7 us
  transfers between devices with their start and end apart: 2, of which 2 were waited for; matrix products, arithmetic and copies ran while one was open for 0% of the time, Pallas kernels for 0%

profile of v1, /device:TPU:8, one launch (start us, length us, event | category | flops | bytes accessed | tf_op | source)
XLA Modules:
  0.0 230.4 jit_solution(6997918503019088035)
XLA Ops:
  6.5 0.0 copy-start
  6.5 0.0 all-gather.2.cloned.1.call-start
  6.5 0.7 all-gather.2.cloned.1.call-update
  7.3 0.0 reduce-scatter.2.cloned.1.call-start
  7.3 19.5 %all_gather.10 = f32[2048,8]{0,1:T(8,128)S(1)} all-gather(f32[128,8]{0,1:T(8,128)} %param.9), channel_id=1, replica_groups=mesh['rep'=2,'rank'=16] {'rank'}, dimensions={0}, use_global_device_ids=true | all-gather | bytes 69632 | tf_op jit(solution)/shard_map/all_gather | solution.py:14
  26.8 18.0 %all_gather.9 = s32[2048,8]{0,1:T(8,128)S(1)} all-gather(s32[128,8]{0,1:T(8,128)} %param.8), channel_id=1, replica_groups=mesh['rep'=2,'rank'=16] {'rank'}, dimensions={0}, use_global_device_ids=true | all-gather | bytes 69632 | tf_op jit(solution)/shard_map/all_gather | solution.py:13
  44.9 40.4 %all-gather.2.cloned.1.call-done = bf16[2048,2048]{1,0:T(8,128)(2,1)} async-done(((bf16[128,2048]{1,0:T(8,128)(2,1)}), bf16[2048,2048]{1,0:T(8,128)(2,1)}) %all-gather.2.cloned.1.call-update) | async-done | bytes 8388624 | tf_op jit(solution)/shard_map/all_gather | solution.py:12
  85.3 11.7 %fusion.3 = f32[2048,768]{1,0:T(8,128)} fusion(bf16[2048,2048]{1,0:T(8,128)(2,1)} %all-gather.2.cloned.1.call-done, bf16[1,2048,768]{2,1,0:T(8,128)(2,1)} %param.11), kind=kOutput, calls=%fused_computation.4 | convolution fusion | flops 6442450944 | bytes 17825792 | tf_op jit(solution)/shard_map/dot_general | solution.py:17
  97.0 0.0 copy-done
  97.0 20.6 %multiply_convert_fusion = bf16[2048,2048]{1,0:T(8,128)(2,1)} fusion(f32[2048]{0:T(1024)S(1)} %select_reduce_fusion, f32[2048,768]{1,0:T(8,128)} %fusion.3, bf16[2048,2048]{1,0:T(8,128)(2,1)} %all-gather.2.cloned.1.call-done, bf16[1,768,2048]{2,1,0:T(8,128)(2,1)S(1)} %copy-done, bf16[1,2048,768]{2,1,0:T(8,128)(2,1)} %param.12), kind=kOutput, calls=%fused_computation | convolution fusion | flops 12902727680 | bytes 29368320 | tf_op jit(solution)/shard_map/dot_general | solution.py:20
  117.6 0.0 copy-start.1
  117.6 0.0 reduce-scatter.2.cloned.1.call-update
  117.6 0.6 copy-done.1
  118.3 0.1 broadcast_add_fusion
  118.3 0.1 eq.21
  118.4 103.0 %reduce-scatter.2.cloned.1.call-done = bf16[128,2048]{1,0:T(8,128)(2,1)} async-done(((bf16[2048,2048]{1,0:T(8,128)(2,1)}), bf16[128,2048]{1,0:T(8,128)(2,1)}) %reduce-scatter.2.cloned.1.call-update) | async-done | bytes 524304 | tf_op jit(solution)/shard_map/reduce_scatter | solution.py:22
  221.4 2.2 convolution_convert_fusion
  (2 shorter events, 0.0 us)
Async XLA Ops:
  6.5 90.4 %copy-start = (bf16[1,768,2048]{2,1,0:T(8,128)(2,1)S(1)}, bf16[1,768,2048]{2,1,0:T(8,128)(2,1)}, u32[]{:S(2)}) copy-start(bf16[1,768,2048]{2,1,0:T(8,128)(2,1)} %param.13) | copy-start | bytes 9437188
  6.5 78.7 %all-gather.2.cloned.1.call-start = ((), (), s32[]{:S(2)}) async-start(), calls=%async_computation.1 | async-start | bytes 8912896 | tf_op jit(solution)/shard_map/all_gather | solution.py:12
  7.3 214.2 %reduce-scatter.2.cloned.1.call-start = ((), (), s32[]{:S(2)}) async-start(), calls=%async_computation.2 | async-start | bytes 8912896 | tf_op jit(solution)/shard_map/reduce_scatter | solution.py:22
  117.6 0.7 copy-start.1
Sparse Core Ops, SparseCore 0:
  9.5 75.7 all-gather.1
  117.7 103.6 reduce-scatter.1

commit v2 on v1

v2 whole, which is shorter than its diff:
```python
import functools

import jax
import jax.numpy as jnp
from jax import lax
from jax.experimental import pallas as pl
from jax.experimental.pallas import tpu as pltpu
from jax.sharding import PartitionSpec as P

MESH = pl.DeviceIdType.MESH


def kernel(
    n, tokens, table, w_gate, w_up, w_down, out,
    held, factors, part, from_core, from_y, from_z, gate_v, up_v, down_v, hidden,
    own_sem, w_sem, f_send, f_recv, ag_send, ag_recv,
    core_send, core_recv, y_send, y_recv, z_send, z_recv, out_sem,
):
    depth = n // 4
    rows, features = tokens.shape
    width = gate_v.shape[1]
    me = lax.axis_index("rank")
    z, y, c = me // 4, (me // 2) % 2, me % 2
    sibling = me + 1 - 2 * c
    across = me + 2 - 4 * y

    own = pltpu.make_async_copy(tokens, held.at[me], own_sem)
    own.start()
    loads = [
        pltpu.make_async_copy(a, b, w_sem.at[i])
        for i, (a, b) in enumerate(((w_gate, gate_v), (w_up, up_v), (w_down, down_v)))
    ]
    for load in loads:
        load.start()

    barrier = pltpu.get_barrier_semaphore()

    @pl.loop(1, n)
    def _(i):
        pl.semaphore_signal(barrier, inc=1, device_id={"rank": (me + i) % n}, device_id_type=MESH)

    pl.semaphore_wait(barrier, n - 1)

    def order(k):
        near = jnp.minimum(z, depth - 1 - z)
        step = (k + 1) // 2
        both = jnp.where(k % 2 == 1, z + step, z - step)
        one = jnp.where(z <= depth - 1 - z, k, depth - 1 - k)
        return jnp.where(k <= 2 * near, both, one)

    def remote(source, target, send, recv, to):
        return pltpu.make_async_remote_copy(
            src_ref=source, dst_ref=target, send_sem=send, recv_sem=recv,
            device_id={"rank": to}, device_id_type=MESH,
        )

    def shard(b, way, to):
        return remote(held.at[b], held.at[b], ag_send.at[way, b], ag_recv.at[b], to)

    def weight(to, source):
        return remote(table.at[to], factors.at[source], f_send.at[to], f_recv.at[source], to)

    def half(pair, side):
        b = 2 * pair + side
        return remote(part.at[b], from_core.at[pair], core_send.at[pair], core_recv.at[pair], sibling)

    def cross(zo):
        return remote(
            part.at[zo * 4 + (1 - y) * 2 + c], from_y.at[zo], y_send.at[zo], y_recv.at[zo], across
        )

    def along(zo, way, to):
        return remote(
            part.at[zo * 4 + y * 2 + c], from_z.at[way, zo], z_send.at[zo], z_recv.at[way, zo], to
        )

    def forward(k):
        zo = order(k)
        b = zo * 4 + y * 2 + c

        @pl.when(zo != z)
        def _():
            shard(b, 0, me).wait_recv()

        @pl.when((zo <= z) & (z < depth - 1))
        def _():
            shard(b, 0, me + 4).start()

        @pl.when((zo >= z) & (z > 0))
        def _():
            shard(b, 1, me - 4).start()

        shard(b, 2, across).start()
        shard(b, 3, sibling).start()

    def expert(pair):
        x = held[pl.ds(2 * pair, 2)].reshape(2 * rows, features)

        @pl.loop(0, width // 256)
        def _(i):
            cols = pl.ds(pl.multiple_of(i * 256, 256), 256)
            g = jnp.dot(x, gate_v[:, cols], preferred_element_type=jnp.float32)
            u = jnp.dot(x, up_v[:, cols], preferred_element_type=jnp.float32)
            hidden[:, cols] = (g / (1.0 + jnp.exp(-g)) * u).astype(jnp.bfloat16)

        eye = lax.broadcasted_iota(jnp.int32, (rows, rows), 0) == lax.broadcasted_iota(
            jnp.int32, (rows, rows), 1
        )
        scale = jnp.concatenate(
            [
                jnp.sum(jnp.where(eye, factors[2 * pair + s][0:1, :], 0.0), axis=1, keepdims=True)
                for s in range(2)
            ],
            axis=0,
        )

        @pl.loop(0, features // 512)
        def _(i):
            cols = pl.ds(pl.multiple_of(i * 512, 512), 512)
            o = jnp.dot(hidden[...], down_v[:, cols], preferred_element_type=jnp.float32)
            o = (o * scale).astype(jnp.bfloat16)
            part[pl.ds(2 * pair, 2), :, cols] = o.reshape(2, rows, 512)

    def add(b, terms):
        @pl.loop(0, rows // 16)
        def _(i):
            r = pl.ds(pl.multiple_of(i * 16, 16), 16)
            total = part[b, r, :].astype(jnp.float32)
            for term in terms:
                total += term[r, :].astype(jnp.float32)
            part[b, r, :] = total.astype(jnp.bfloat16)

    def reduce_pairs(k):
        zo = order(k)
        for yo in (1 - y, y):
            pair = 2 * zo + yo
            half(pair, c).wait_recv()
            add(2 * pair + c, [from_core.at[pair]])
            if yo is not y:
                cross(zo).start()

    @pl.loop(1, n)
    def _(i):
        weight((me + i) % n, me).start()

    mine = pltpu.make_async_copy(table.at[me], factors.at[me], f_send.at[me])
    mine.start()
    own.wait()
    forward(0)
    mine.wait()
    for load in loads:
        load.wait()

    @pl.loop(1, n)
    def _(i):
        weight(me, (me + i) % n).wait_recv()

    @pl.loop(0, depth)
    def _(k):
        zo = order(k)
        shard(zo * 4 + y * 2 + 1 - c, 3, sibling).wait_recv()
        expert(2 * zo + y)
        half(2 * zo + y, 1 - c).start()

        @pl.when(k < depth - 1)
        def _():
            forward(k + 1)

        @pl.when(k > 0)
        def _():
            reduce_pairs(k - 1)

        b = zo * 4 + (1 - y) * 2 + c
        shard(b, 2, across).wait_recv()
        shard(b, 3, sibling).start()
        shard(b + 1 - 2 * c, 3, sibling).wait_recv()
        expert(2 * zo + 1 - y)
        half(2 * zo + 1 - y, 1 - c).start()

    reduce_pairs(depth - 1)

    @pl.loop(0, depth)
    def _(i):
        zo = order(depth - 1 - i)
        b = zo * 4 + y * 2 + c
        cross(zo).wait_recv()
        add(b, [from_y.at[zo]])

        @pl.when((zo >= z) & (z > 0))
        def _():
            along(zo, 0, me).wait_recv()
            add(b, [from_z.at[0, zo]])

        @pl.when((zo <= z) & (z < depth - 1))
        def _():
            along(zo, 1, me).wait_recv()
            add(b, [from_z.at[1, zo]])

        @pl.when(zo > z)
        def _():
            along(zo, 0, me + 4).start()

        @pl.when(zo < z)
        def _():
            along(zo, 1, me - 4).start()

    done = pltpu.make_async_copy(part.at[me], out, out_sem)
    done.start()

    @pl.loop(1, n)
    def _(i):
        weight((me + i) % n, me).wait_send()

    @pl.loop(0, depth)
    def _(zo):
        b = zo * 4 + y * 2 + c

        @pl.when((zo <= z) & (z < depth - 1))
        def _():
            shard(b, 0, me + 4).wait_send()

        @pl.when((zo >= z) & (z > 0))
        def _():
            shard(b, 1, me - 4).wait_send()

        shard(b, 2, across).wait_send()
        shard(b, 3, sibling).wait_send()
        shard(zo * 4 + (1 - y) * 2 + c, 3, sibling).wait_send()
        half(2 * zo, 1 - c).wait_send()
        half(2 * zo + 1, 1 - c).wait_send()
        cross(zo).wait_send()

        @pl.when(zo > z)
        def _():
            along(zo, 0, me + 4).wait_send()

        @pl.when(zo < z)
        def _():
            along(zo, 1, me - 4).wait_send()

    done.wait()


def exchange(n, tokens, table, w_gate, w_up, w_down):
    rows, features = tokens.shape
    width = w_gate.shape[1]
    depth = n // 4
    bf, dma = jnp.bfloat16, pltpu.SemaphoreType.DMA
    return pl.pallas_call(
        functools.partial(kernel, n),
        out_shape=jax.ShapeDtypeStruct((rows, features), bf),
        in_specs=[
            pl.BlockSpec(memory_space=pl.ANY),
            pl.BlockSpec(memory_space=pltpu.VMEM),
            pl.BlockSpec(memory_space=pl.ANY),
            pl.BlockSpec(memory_space=pl.ANY),
            pl.BlockSpec(memory_space=pl.ANY),
        ],
        out_specs=pl.BlockSpec(memory_space=pl.ANY),
        scratch_shapes=[
            pltpu.VMEM((n, rows, features), bf),
            pltpu.VMEM((n, 8, rows), jnp.float32),
            pltpu.VMEM((n, rows, features), bf),
            pltpu.VMEM((n // 2, rows, features), bf),
            pltpu.VMEM((depth, rows, features), bf),
            pltpu.VMEM((2, depth, rows, features), bf),
            pltpu.VMEM((features, width), bf),
            pltpu.VMEM((features, width), bf),
            pltpu.VMEM((width, features), bf),
            pltpu.VMEM((2 * rows, width), bf),
            dma, dma((3,)), dma((n,)), dma((n,)), dma((4, n)), dma((n,)),
            dma((n // 2,)), dma((n // 2,)), dma((depth,)), dma((depth,)),
            dma((depth,)), dma((2, depth)), dma,
        ],
        compiler_params=pltpu.CompilerParams(
            collective_id=0, has_side_effects=True, vmem_limit_bytes=56 * 1024 * 1024
        ),
        cost_estimate=pl.CostEstimate(
            flops=6 * n * rows * features * width,
            bytes_accessed=6 * features * width + 4 * rows * features,
            transcendentals=n * rows * width,
        ),
    )(tokens, table, w_gate, w_up, w_down)


def collectives(tokens, routes, gate_weights, w_gate, w_up, w_down):
    rank = lax.axis_index("rank")
    everyone = lax.all_gather(tokens, "rank", axis=0, tiled=True)
    all_routes = lax.all_gather(routes, "rank", axis=0, tiled=True)
    all_gates = lax.all_gather(gate_weights, "rank", axis=0, tiled=True)
    factor = jnp.sum(jnp.where(all_routes == rank, all_gates, 0.0), axis=1)
    gate_proj = jnp.dot(everyone, w_gate, preferred_element_type=jnp.float32)
    up_proj = jnp.dot(everyone, w_up, preferred_element_type=jnp.float32)
    hidden = (jax.nn.silu(gate_proj) * up_proj).astype(jnp.bfloat16)
    expert_out = jnp.dot(hidden, w_down, preferred_element_type=jnp.float32)
    weighed = (factor[:, None] * expert_out).astype(jnp.bfloat16)
    return lax.psum_scatter(weighed, "rank", scatter_dimension=0, tiled=True)


def per_device(tokens, routes, gate_weights, token_order, w_gate, w_up, w_down):
    n = lax.axis_size("rank")
    rows, features = tokens.shape
    blocks, block_rows = token_order.shape
    own_weights = (w_gate[0], w_up[0], w_down[0])

    if n % 4 == 0 and n * rows * features <= 4 * 1024 * 1024:
        chosen = routes.T[None] == jnp.arange(n, dtype=jnp.int32)[:, None, None]
        table = jnp.sum(jnp.where(chosen, gate_weights.T[None], 0.0), axis=1)
        table = jnp.broadcast_to(table[:, None, :], (n, 8, rows))
        combined = exchange(n, tokens, table, *own_weights)
    else:
        combined = collectives(tokens, routes, gate_weights, *own_weights)

    order = token_order + jnp.arange(blocks, dtype=jnp.int32)[:, None] * block_rows
    pick = (order.reshape(-1)[:, None] == jnp.arange(rows, dtype=jnp.int32)[None, :])
    return jnp.dot(
        pick.astype(jnp.bfloat16), combined, preferred_element_type=jnp.float32
    ).astype(jnp.bfloat16)


def solution(mesh):
    return jax.shard_map(
        per_device,
        mesh=mesh,
        in_specs=(
            P(("rep", "rank"), None),
            P(("rep", "rank"), None),
            P(("rep", "rank"), None),
            P(("rep", "rank"), None),
            P("rank", None, None),
            P("rank", None, None),
            P("rank", None, None),
        ),
        out_specs=P(("rep", "rank"), None),
        check_vma=False,
    )
```

time: 232 us -> 157 us (0.68)
  Pallas kernels: 0 us -> 150 us
  waiting for transfers between devices: 144 us -> 0 us
  blocking collectives: 37.6 us -> 0 us
  matrix products: 34.5 us -> 2.18 us
  between operations: 13.4 us -> 0.01 us
    pallas_call x0 -> x1, Pallas kernels: none -> 150 us  [exchange(): pl.pallas_call(functools.partial(kernel, n), out_shape=jax.ShapeDtypeStru...]
    reduce_scatter x1 -> x0, waiting for transfers between devices: 103 us -> none  [per_device(): lax.psum_scatter(weighed, 'rank', scatter_dimension=0, tiled=True)]
    all_gather x1 -> x0, waiting for transfers between devices: 40.4 us -> none  [per_device(): everyone = lax.all_gather(tokens, 'rank', axis=0, tiled=True)]
    all_gather x2 -> x0, blocking collectives: 37.6 us -> none  [the longest x1 19.5 us: per_device(): all_gates = lax.all_gather(gate_weights, 'rank', axis=0, tiled=True)]
    dot_general x2 -> x0, matrix products: 32.3 us -> none  [the longest x1 20.6 us: per_device(): expert_out = jnp.dot(hidden, w_down[0], preferred_element_type=jnp.float32)]
  transfers between devices with their start and end apart: 2 -> 0, of which waited for: 2 -> 0; matrix products, arithmetic and copies ran while one was open for 0% -> 0% of each run, Pallas kernels for 0% -> 0%
where the time goes in v2:
time: 157 us; the launch traced here: 155 us
  Pallas kernels  150 us (96%)
  matrix products  2.18 us (1%)
    pallas_call x1, Pallas kernels, exchange(): pl.pallas_call(functools.partial(kernel, n), out_shape=jax.ShapeDtypeStru...  150 us

profile of v2, /device:TPU:8, one launch (start us, length us, event | category | flops | bytes accessed | tf_op | source)
XLA Modules:
  0.0 154.8 jit_solution(909613043707448240)
XLA Ops:
  0.0 0.8 broadcast_add_fusion
  0.8 0.1 eq.28
  0.8 0.7 select_reduce_fusion
  1.6 0.6 broadcast_in_dim.16.table
  2.2 150.4 %shard_map.73 = bf16[128,2048]{1,0:T(8,128)(2,1)} custom-call(bf16[128,2048]{1,0:T(8,128)(2,1)} %tokens.1, f32[16,8,128]{2,1,0:T(8,128)} %broadcast_in_dim.16.table, bf16[2048,768]{1,0:T(8,128)(2,1)} %bitcast.8, bf16[2048,768]{1,0:T(8,128)(2,1)} %bitcast.9, bf16[768,2048]{1,0:T(8,128)(2,1)} %bitcast.10), custom_call_target="tpu_custom_call" | custom-call | flops 19327352832 | bytes 10485760 | tf_op jit(solution)/shard_map/pallas_call | solution.py:249
  152.6 2.2 %convolution_convert_fusion = bf16[128,2048]{1,0:T(8,128)(2,1)} fusion(bf16[128,2048]{1,0:T(8,128)(2,1)} %shard_map.73, s32[128]{0:T(128)S(1)} %eq.28), kind=kOutput, calls=%fused_computation | convolution fusion | flops 67387392 | bytes 1049088 | tf_op jit(solution)/shard_map/dot_general | solution.py:316
  (1 shorter events, 0.0 us)

commit v3 on v2

--- a/solution.py
+++ b/solution.py
@@ -8,6 +8,7 @@
 from jax.sharding import PartitionSpec as P
 
 MESH = pl.DeviceIdType.MESH
+CHUNKS = 2
 
 
 def kernel(
@@ -44,8 +45,9 @@
     def order(k):
         near = jnp.minimum(z, depth - 1 - z)
         step = (k + 1) // 2
-        both = jnp.where(k % 2 == 1, z + step, z - step)
-        one = jnp.where(z <= depth - 1 - z, k, depth - 1 - k)
+        low = z <= depth - 1 - z
+        both = jnp.where((k % 2 == 1) == low, z + step, z - step)
+        one = jnp.where(low, k, depth - 1 - k)
         return jnp.where(k <= 2 * near, both, one)
 
     def remote(source, target, send, recv, to):
@@ -64,14 +66,19 @@
         b = 2 * pair + side
         return remote(part.at[b], from_core.at[pair], core_send.at[pair], core_recv.at[pair], sibling)
 
-    def cross(zo):
+    def chunk(h):
+        return pl.ds(h * (rows // CHUNKS), rows // CHUNKS)
+
+    def cross(zo, h):
         return remote(
-            part.at[zo * 4 + (1 - y) * 2 + c], from_y.at[zo], y_send.at[zo], y_recv.at[zo], across
-        )
-
-    def along(zo, way, to):
+            part.at[zo * 4 + (1 - y) * 2 + c, chunk(h)], from_y.at[zo, chunk(h)],
+            y_send.at[zo, h], y_recv.at[zo, h], across,
+        )
+
+    def along(zo, way, h, to):
         return remote(
-            part.at[zo * 4 + y * 2 + c], from_z.at[way, zo], z_send.at[zo], z_recv.at[way, zo], to
+            part.at[zo * 4 + y * 2 + c, chunk(h)], from_z.at[way, zo, chunk(h)],
+            z_send.at[zo, h], z_recv.at[way, zo, h], to,
         )
 
     def forward(k):
@@ -121,13 +128,13 @@
             o = (o * scale).astype(jnp.bfloat16)
             part[pl.ds(2 * pair, 2), :, cols] = o.reshape(2, rows, 512)
 
-    def add(b, terms):
-        @pl.loop(0, rows // 16)
+    def add(b, term, h):
+        size = rows // CHUNKS
+
+        @pl.loop(0, size // 16)
         def _(i):
-            r = pl.ds(pl.multiple_of(i * 16, 16), 16)
-            total = part[b, r, :].astype(jnp.float32)
-            for term in terms:
-                total += term[r, :].astype(jnp.float32)
+            r = pl.ds(pl.multiple_of(h * size + i * 16, 16), 16)
+            total = part[b, r, :].astype(jnp.float32) + term[r, :].astype(jnp.float32)
             part[b, r, :] = total.astype(jnp.bfloat16)
 
     def reduce_pairs(k):
@@ -135,9 +142,10 @@
         for yo in (1 - y, y):
             pair = 2 * zo + yo
             half(pair, c).wait_recv()
-            add(2 * pair + c, [from_core.at[pair]])
-            if yo is not y:
-                cross(zo).start()
+            for h in range(CHUNKS):
+                add(2 * pair + c, from_core.at[pair], h)
+                if yo is not y:
+                    cross(zo, h).start()
 
     @pl.loop(1, n)
     def _(i):
@@ -166,9 +174,11 @@
         def _():
             forward(k + 1)
 
-        @pl.when(k > 0)
-        def _():
-            reduce_pairs(k - 1)
+        if depth > 3:
+
+            @pl.when(k == depth - 1)
+            def _():
+                reduce_pairs(1)
 
         b = zo * 4 + (1 - y) * 2 + c
         shard(b, 2, across).wait_recv()
@@ -177,32 +187,40 @@
         expert(2 * zo + 1 - y)
         half(2 * zo + 1 - y, 1 - c).start()
 
-    reduce_pairs(depth - 1)
+    last = [k for k in reversed(range(depth)) if depth < 4 or k != 1]
+
+    @pl.loop(0, len(last))
+    def _(i):
+        reduce_pairs(jnp.where(i == len(last) - 1, 0, depth - 1 - i))
 
     @pl.loop(0, depth)
     def _(i):
-        zo = order(depth - 1 - i)
+        ends = jnp.where(i == depth - 1, 0, jnp.where(i == 0, 1, depth - i))
+        zo = order(jnp.where((z == 0) | (z == depth - 1), ends, depth - 1 - i))
         b = zo * 4 + y * 2 + c
-        cross(zo).wait_recv()
-        add(b, [from_y.at[zo]])
-
-        @pl.when((zo >= z) & (z > 0))
-        def _():
-            along(zo, 0, me).wait_recv()
-            add(b, [from_z.at[0, zo]])
-
-        @pl.when((zo <= z) & (z < depth - 1))
-        def _():
-            along(zo, 1, me).wait_recv()
-            add(b, [from_z.at[1, zo]])
-
-        @pl.when(zo > z)
-        def _():
-            along(zo, 0, me + 4).start()
-
-        @pl.when(zo < z)
-        def _():
-            along(zo, 1, me - 4).start()
+
+        @pl.loop(0, CHUNKS)
+        def _(h):
+            cross(zo, h).wait_recv()
+            add(b, from_y.at[zo], h)
+
+            @pl.when((zo >= z) & (z > 0))
+            def _():
+                along(zo, 0, h, me).wait_recv()
+                add(b, from_z.at[0, zo], h)
+
+            @pl.when((zo <= z) & (z < depth - 1))
+            def _():
+                along(zo, 1, h, me).wait_recv()
+                add(b, from_z.at[1, zo], h)
+
+            @pl.when(zo > z)
+            def _():
+                along(zo, 0, h, me + 4).start()
+
+            @pl.when(zo < z)
+            def _():
+                along(zo, 1, h, me - 4).start()
 
     done = pltpu.make_async_copy(part.at[me], out, out_sem)
     done.start()
@@ -228,15 +246,18 @@
         shard(zo * 4 + (1 - y) * 2 + c, 3, sibling).wait_send()
         half(2 * zo, 1 - c).wait_send()
         half(2 * zo + 1, 1 - c).wait_send()
-        cross(zo).wait_send()
+        for h in range(CHUNKS):
+            cross(zo, h).wait_send()
 
         @pl.when(zo > z)
         def _():
-            along(zo, 0, me + 4).wait_send()
+            for h in range(CHUNKS):
+                along(zo, 0, h, me + 4).wait_send()
 
         @pl.when(zo < z)
         def _():
-            along(zo, 1, me - 4).wait_send()
+            for h in range(CHUNKS):
+                along(zo, 1, h, me - 4).wait_send()
 
     done.wait()
 
@@ -269,8 +290,8 @@
             pltpu.VMEM((width, features), bf),
             pltpu.VMEM((2 * rows, width), bf),
             dma, dma((3,)), dma((n,)), dma((n,)), dma((4, n)), dma((n,)),
-            dma((n // 2,)), dma((n // 2,)), dma((depth,)), dma((depth,)),
-            dma((depth,)), dma((2, depth)), dma,
+            dma((n // 2,)), dma((n // 2,)), dma((depth, CHUNKS)), dma((depth, CHUNKS)),
+            dma((depth, CHUNKS)), dma((2, depth, CHUNKS)), dma,
         ],
         compiler_params=pltpu.CompilerParams(
             collective_id=0, has_side_effects=True, vmem_limit_bytes=56 * 1024 * 1024
@@ -303,7 +324,7 @@
     blocks, block_rows = token_order.shape
     own_weights = (w_gate[0], w_up[0], w_down[0])
 
-    if n % 4 == 0 and n * rows * features <= 4 * 1024 * 1024:
+    if n % 4 == 0 and n <= 16 and n * rows * features <= 4 * 1024 * 1024:
         chosen = routes.T[None] == jnp.arange(n, dtype=jnp.int32)[:, None, None]
         table = jnp.sum(jnp.where(chosen, gate_weights.T[None], 0.0), axis=1)
         table = jnp.broadcast_to(table[:, None, :], (n, 8, rows))

time: 157 us -> 126 us (0.80); the launches traced: 155 us -> 126 us
  Pallas kernels: 150 us -> 122 us
    pallas_call x1, Pallas kernels: 150 us -> 122 us  [exchange(): pl.pallas_call(functools.partial(kernel, n), out_shape=jax.ShapeDtypeStru...]
where the time goes in v3:
time: 126 us
  Pallas kernels  122 us (97%)
  matrix products  2.18 us (2%)
  other arithmetic  1.48 us (1%)
    pallas_call x1, Pallas kernels, exchange(): pl.pallas_call(functools.partial(kernel, n), out_shape=jax.ShapeDtypeStru...  122 us

profile of v3, /device:TPU:8, one launch (start us, length us, event | category | flops | bytes accessed | tf_op | source)
XLA Modules:
  0.0 126.2 jit_solution(6886175612960363111)
XLA Ops:
  0.0 0.8 broadcast_add_fusion
  0.8 0.1 eq.28
  0.8 0.7 select_reduce_fusion
  1.6 0.6 broadcast_in_dim.16.table
  2.2 121.8 %shard_map.73 = bf16[128,2048]{1,0:T(8,128)(2,1)} custom-call(bf16[128,2048]{1,0:T(8,128)(2,1)} %tokens.1, f32[16,8,128]{2,1,0:T(8,128)} %broadcast_in_dim.16.table, bf16[2048,768]{1,0:T(8,128)(2,1)} %bitcast.8, bf16[2048,768]{1,0:T(8,128)(2,1)} %bitcast.9, bf16[768,2048]{1,0:T(8,128)(2,1)} %bitcast.10), custom_call_target="tpu_custom_call" | custom-call | flops 19327352832 | bytes 10485760 | tf_op jit(solution)/shard_map/pallas_call | solution.py:270
  124.0 2.2 %convolution_convert_fusion = bf16[128,2048]{1,0:T(8,128)(2,1)} fusion(bf16[128,2048]{1,0:T(8,128)(2,1)} %shard_map.73, s32[128]{0:T(128)S(1)} %eq.28), kind=kOutput, calls=%fused_computation | convolution fusion | flops 67387392 | bytes 1049088 | tf_op jit(solution)/shard_map/dot_general | solution.py:337
  (1 shorter events, 0.0 us)

commit v4 on v3

--- a/solution.py
+++ b/solution.py
@@ -8,7 +8,7 @@
 from jax.sharding import PartitionSpec as P
 
 MESH = pl.DeviceIdType.MESH
-CHUNKS = 2
+CHUNKS = 4
 
 
 def kernel(

time: 126 us -> 125 us (level)
  Pallas kernels: 122 us -> 120 us
    pallas_call x1, Pallas kernels: 122 us -> 120 us  [exchange(): pl.pallas_call(functools.partial(kernel, n), out_shape=jax.ShapeDtypeStru...]
where the time goes in v4:
time: 125 us
  Pallas kernels  120 us (96%)
  matrix products  2.18 us (2%)
  other arithmetic  1.48 us (1%)
    pallas_call x1, Pallas kernels, exchange(): pl.pallas_call(functools.partial(kernel, n), out_shape=jax.ShapeDtypeStru...  120 us

profile of v4, /device:TPU:8, one launch (start us, length us, event | category | flops | bytes accessed | tf_op | source)
XLA Modules:
  0.0 124.6 jit_solution(4541405591386686212)
XLA Ops:
  0.0 0.8 broadcast_add_fusion
  0.8 0.1 eq.28
  0.8 0.7 select_reduce_fusion
  1.6 0.6 broadcast_in_dim.16.table
  2.2 120.2 %shard_map.73 = bf16[128,2048]{1,0:T(8,128)(2,1)} custom-call(bf16[128,2048]{1,0:T(8,128)(2,1)} %tokens.1, f32[16,8,128]{2,1,0:T(8,128)} %broadcast_in_dim.16.table, bf16[2048,768]{1,0:T(8,128)(2,1)} %bitcast.8, bf16[2048,768]{1,0:T(8,128)(2,1)} %bitcast.9, bf16[768,2048]{1,0:T(8,128)(2,1)} %bitcast.10), custom_call_target="tpu_custom_call" | custom-call | flops 19327352832 | bytes 10485760 | tf_op jit(solution)/shard_map/pallas_call | solution.py:270
  122.4 2.2 %convolution_convert_fusion = bf16[128,2048]{1,0:T(8,128)(2,1)} fusion(bf16[128,2048]{1,0:T(8,128)(2,1)} %shard_map.73, s32[128]{0:T(128)S(1)} %eq.28), kind=kOutput, calls=%fused_computation | convolution fusion | flops 67387392 | bytes 1049088 | tf_op jit(solution)/shard_map/dot_general | solution.py:337
  (1 shorter events, 0.0 us)

commit v5 on v4

--- a/solution.py
+++ b/solution.py
@@ -147,14 +147,15 @@
                 if yo is not y:
                     cross(zo, h).start()
 
+    own.wait()
+    forward(0)
+
     @pl.loop(1, n)
     def _(i):
         weight((me + i) % n, me).start()
 
     mine = pltpu.make_async_copy(table.at[me], factors.at[me], f_send.at[me])
     mine.start()
-    own.wait()
-    forward(0)
     mine.wait()
     for load in loads:
         load.wait()

time: 125 us -> 130 us (1.040)
  Pallas kernels: 120 us -> 126 us
    pallas_call x1, Pallas kernels: 120 us -> 126 us  [exchange(): pl.pallas_call(functools.partial(kernel, n), out_shape=jax.ShapeDtypeStru...]
where the time goes in v5:
time: 130 us
  Pallas kernels  126 us (97%)
  matrix products  2.18 us (2%)
  other arithmetic  1.48 us (1%)
    pallas_call x1, Pallas kernels, exchange(): pl.pallas_call(functools.partial(kernel, n), out_shape=jax.ShapeDtypeStru...  126 us

profile of v5, /device:TPU:8, one launch (start us, length us, event | category | flops | bytes accessed | tf_op | source)
XLA Modules:
  0.0 129.9 jit_solution(17594033113472801302)
XLA Ops:
  0.0 0.8 broadcast_add_fusion
  0.8 0.1 eq.28
  0.8 0.7 select_reduce_fusion
  1.6 0.6 broadcast_in_dim.16.table
  2.2 125.5 %shard_map.73 = bf16[128,2048]{1,0:T(8,128)(2,1)} custom-call(bf16[128,2048]{1,0:T(8,128)(2,1)} %tokens.1, f32[16,8,128]{2,1,0:T(8,128)} %broadcast_in_dim.16.table, bf16[2048,768]{1,0:T(8,128)(2,1)} %bitcast.8, bf16[2048,768]{1,0:T(8,128)(2,1)} %bitcast.9, bf16[768,2048]{1,0:T(8,128)(2,1)} %bitcast.10), custom_call_target="tpu_custom_call" | custom-call | flops 19327352832 | bytes 10485760 | tf_op jit(solution)/shard_map/pallas_call | solution.py:271
  127.7 2.2 %convolution_convert_fusion = bf16[128,2048]{1,0:T(8,128)(2,1)} fusion(bf16[128,2048]{1,0:T(8,128)(2,1)} %shard_map.73, s32[128]{0:T(128)S(1)} %eq.28), kind=kOutput, calls=%fused_computation | convolution fusion | flops 67387392 | bytes 1049088 | tf_op jit(solution)/shard_map/dot_general | solution.py:338
  (1 shorter events, 0.0 us)
